TPU v7x, 128 devices: a whole 4x4x4 slice. The times are simulated.
128 devices in a mesh: gx: 4 (over x), yz: 32 (over y, z, core).
Axes of the slice: x: 4, y: 4, z: 4, core: 2. Of those that a mesh axis runs over, the one named last changes fastest.
Arguments:
- tokens: bfloat16 [512, 12288], P(None, ('gx', 'yz')), may hold values from -24 to 24
- gate_weight: bfloat16 [12288, 40960], P('gx', 'yz'), may hold values from -0.0546875 to 0.0546875
- up_weight: bfloat16 [12288, 40960], P('gx', 'yz'), may hold values from -0.0546875 to 0.0546875
- down_weight: bfloat16 [40960, 12288], P('yz', 'gx'), may hold values from -0.0546875 to 0.0546875
Outputs:
- mixed: bfloat16 [512, 12288], P(None, ('gx', 'yz'))
All inputs are finite; a program needn't handle non-finite values.
Results may differ from a plain program's by a relative error of at most 0.0049.
Values may be sent and summed in bfloat16 or wider, within the bound.
A program may use at most 128 MiB of HBM per device.

v0:
```python
import jax
import jax.numpy as jnp
from jax import lax
from jax.sharding import PartitionSpec as P


def body(tokens, gate_weight, up_weight, down_weight):
    features = lax.all_gather(tokens, "yz", axis=1, tiled=True)
    width = gate_weight.shape[1]
    gate_part = jnp.dot(features, gate_weight, preferred_element_type=jnp.float32)
    up_part = jnp.dot(features, up_weight, preferred_element_type=jnp.float32)
    summed = lax.psum_scatter(
        jnp.concatenate([gate_part, up_part], axis=1), "gx", scatter_dimension=0, tiled=True
    )
    local_hidden = (jax.nn.silu(summed[:, :width]) * summed[:, width:]).astype(jnp.bfloat16)
    hidden = lax.all_gather(local_hidden, "gx", axis=0, tiled=True)
    partial_out = jnp.dot(hidden, down_weight, preferred_element_type=jnp.float32)
    mixed = lax.psum_scatter(partial_out, "yz", scatter_dimension=1, tiled=True)
    return mixed.astype(jnp.bfloat16)


def solution(mesh):
    return jax.shard_map(
        body,
        mesh=mesh,
        in_specs=(P(None, ("gx", "yz")), P("gx", "yz"), P("gx", "yz"), P("yz", "gx")),
        out_specs=P(None, ("gx", "yz")),
        check_vma=False,
    )
```

profile of v0, /device:TPU:1, one launch (start us, length us, event | category | flops | bytes accessed | tf_op | source)
XLA Modules:
  0.0 262.7 jit_solution(10002435762999765800)
XLA Ops:
  6.5 0.0 all-gather.3.cloned.1.call-start
  6.5 0.7 all-gather.3.cloned.1.call-update
  7.3 0.0 reduce-scatter.3.cloned.1.call-start
  7.3 51.2 %all-gather.3.cloned.1.call-done = bf16[512,3072]{0,1:T(8,128)(2,1)} async-done(((bf16[512,96]{0,1:T(8,128)(2,1)}), bf16[512,3072]{0,1:T(8,128)(2,1)}) %all-gather.3.cloned.1.call-update) | async-done | bytes 3145744 | tf_op jit(solution)/shard_map/all_gather | solution.py:8
  58.5 0.0 copy-start
  58.5 8.8 %fusion.2 = f32[512,1280]{1,0:T(8,128)S(1)} fusion(bf16[512,3072]{0,1:T(8,128)(2,1)} %all-gather.3.cloned.1.call-done, bf16[3072,1280]{1,0:T(8,128)(2,1)} %param.6), kind=kOutput, calls=%fused_computation.4 | convolution fusion | flops 4026531840 | bytes 13631488 | tf_op jit(solution)/shard_map/dot_general | solution.py:11
  67.3 0.0 copy-done
  67.3 6.8 %fusion.1 = f32[512,1280]{1,0:T(8,128)S(1)} fusion(bf16[512,3072]{0,1:T(8,128)(2,1)S(1)} %copy-done, bf16[3072,1280]{1,0:T(8,128)(2,1)} %param.5), kind=kOutput, calls=%fused_computation.3 | convolution fusion | flops 4026531840 | bytes 13631488 | tf_op jit(solution)/shard_map/dot_general | solution.py:10
  74.1 2.9 %pad_maximum_fusion = f32[512,2560]{1,0:T(8,128)} fusion(f32[512,1280]{1,0:T(8,128)S(1)} %fusion.2, f32[512,1280]{1,0:T(8,128)S(1)} %fusion.1), kind=kLoop, calls=%fused_computation | loop fusion | flops 1310720 | bytes 10485760 | tf_op jit(solution)/shard_map/concatenate | solution.py:13
  77.1 0.0 reduce-scatter.3.cloned.1.call-update
  77.1 0.0 all-gather.5.cloned.1.call-start
  77.1 54.3 %reduce-scatter.3.cloned.1.call-done = f32[128,2560]{1,0:T(8,128)} async-done(((f32[512,2560]{1,0:T(8,128)}), f32[128,2560]{1,0:T(8,128)}) %reduce-scatter.3.cloned.1.call-update) | async-done | bytes 1310736 | tf_op jit(solution)/shard_map/reduce_scatter | solution.py:12
  131.5 2.2 fusion
  133.7 0.0 all-gather.5.cloned.1.call-update
  133.7 0.0 reduce-scatter.5.cloned.1.call-start
  133.7 23.5 %all-gather.5.cloned.1.call-done = bf16[512,1280]{1,0:T(8,128)(2,1)} async-done(((bf16[128,1280]{1,0:T(8,128)(2,1)}), bf16[512,1280]{1,0:T(8,128)(2,1)}) %all-gather.5.cloned.1.call-update) | async-done | bytes 1310736 | tf_op jit(solution)/shard_map/all_gather | solution.py:16
  157.2 10.6 %fusion.3 = f32[512,3072]{0,1:T(8,128)} fusion(bf16[512,1280]{1,0:T(8,128)(2,1)} %all-gather.5.cloned.1.call-done, bf16[1280,3072]{1,0:T(8,128)(2,1)} %param.7), kind=kOutput, calls=%fused_computation.5 | convolution fusion | flops 4026531840 | bytes 15466496 | tf_op jit(solution)/shard_map/dot_general | solution.py:17
  167.8 0.0 reduce-scatter.5.cloned.1.call-update
  167.8 86.7 %reduce-scatter.5.cloned.1.call-done = f32[512,96]{0,1:T(8,128)} async-done(((f32[512,3072]{0,1:T(8,128)}), f32[512,96]{0,1:T(8,128)}) %reduce-scatter.5.cloned.1.call-update) | async-done | bytes 196624 | tf_op jit(solution)/shard_map/reduce_scatter | solution.py:18
  254.5 1.6 convert_element_type.7
Async XLA Ops:
  6.5 52.0 %all-gather.3.cloned.1.call-start = ((), (), s32[]{:S(2)}) async-start(), calls=%async_computation.2 | async-start | bytes 3244032 | tf_op jit(solution)/shard_map/all_gather | solution.py:8
  7.3 124.2 %reduce-scatter.3.cloned.1.call-start = ((), (), s32[]{:S(2)}) async-start(), calls=%async_computation.3 | async-start | bytes 6553600 | tf_op jit(solution)/shard_map/reduce_scatter | solution.py:12
  58.5 8.8 %copy-start = (bf16[512,3072]{0,1:T(8,128)(2,1)S(1)}, bf16[512,3072]{0,1:T(8,128)(2,1)}, u32[]{:S(2)}) copy-start(bf16[512,3072]{0,1:T(8,128)(2,1)} %all-gather.3.cloned.1.call-done) | copy-start | bytes 9437188
  77.1 80.1 %all-gather.5.cloned.1.call-start = ((), (), s32[]{:S(2)}) async-start(), calls=%async_computation.4 | async-start | bytes 1638400 | tf_op jit(solution)/shard_map/all_gather | solution.py:16
  133.7 120.9 %reduce-scatter.5.cloned.1.call-start = ((), (), s32[]{:S(2)}) async-start(), calls=%async_computation.5 | async-start | bytes 6488064 | tf_op jit(solution)/shard_map/reduce_scatter | solution.py:18
Sparse Core Ops, SparseCore 0:
  9.6 48.8 all-gather.2
  77.2 54.2 reduce-scatter.2
  133.8 23.3 all-gather.4
  167.9 86.5 reduce-scatter.4
where the time goes:
time: 264 us; the launch traced here: 263 us
  waiting for transfers between devices  216 us (82%)
  matrix products  26.2 us (10%)
  between operations  13.2 us (5%)
  other arithmetic  6.72 us (3%)
    reduce_scatter x1, waiting for transfers between devices, body(): mixed = lax.psum_scatter(partial_out, 'yz', scatter_dimension=1, tiled=True)  86.7 us
    reduce_scatter x1, waiting for transfers between devices, body(): lax.psum_scatter(jnp.concatenate([gate_part, up_part], axis=1), 'gx', sca...  54.3 us
    all_gather x1, waiting for transfers between devices, body(): features = lax.all_gather(tokens, 'yz', axis=1, tiled=True)  51.2 us
    all_gather x1, waiting for transfers between devices, body(): hidden = lax.all_gather(local_hidden, 'gx', axis=0, tiled=True)  23.5 us
    dot_general x1, matrix products, body(): jnp.dot(hidden, down_weight, preferred_element_type=jnp.float32)  10.6 us
    dot_general x1, matrix products, body(): up_part = jnp.dot(features, up_weight, preferred_element_type=jnp.float32)  8.76 us
    dot_general x1, matrix products, body(): jnp.dot(features, gate_weight, preferred_element_type=jnp.float32)  6.84 us
  transfers between devices with their start and end apart: 4, of which 4 were waited for; matrix products, arithmetic and copies ran while one was open for 0% of the time, Pallas kernels for 0%

commit v1 on v0

v1 whole, which is shorter than its diff:
```python
import jax
import jax.numpy as jnp
from jax import lax
from jax.experimental import pallas as pl
from jax.experimental.pallas import tpu as pltpu
from jax.sharding import PartitionSpec as P

MESH = pl.DeviceIdType.MESH
F32 = jnp.float32
BF16 = jnp.bfloat16

TOK = 512
NC = 4
T = TOK // NC
Q = T // 4
DL = 3072
FL = 1280
NB = 96
CH = 16


def kernel(tok, wg_h, wu_h, wd_h, out,
           wg, wu, wd, xt, xn, pg, pu, sg, su, r1g, r1u, mg, mu, rmg, rmu, rpg, rpu,
           hb, ob, of, sib, sd, sf, rd,
           wsem, a_s, a_r, as_s, as_r, x_s, x_r, d0_s, d0_r, d1_s, d1_r):
    x = lax.axis_index("gx")
    yz = lax.axis_index("yz")
    chip = yz // 2
    k = yz % 2
    y = chip // 4
    z = chip % 4
    xp = (x + 1) % 4
    xm = (x + 3) % 4
    xo = (x + 2) % 4
    sibling = (x, chip * 2 + (1 - k))
    plus = (xp, yz)
    minus = (xm, yz)

    def peer(o):
        return ((y + o // 4) % 4) * 4 + (z + o % 4) % 4

    weights = [pltpu.make_async_copy(h, v, wsem.at[i]) for i, (h, v) in enumerate(((wg_h, wg), (wu_h, wu), (wd_h, wd)))]
    for w in weights:
        w.start()

    barrier = pltpu.get_barrier_semaphore()

    def greet(o, _):
        pl.semaphore_signal(barrier, inc=1, device_id=(x, peer(o) * 2 + k), device_id_type=MESH)
        return 0

    lax.fori_loop(1, CH, greet, 0)
    for dev in (sibling, plus, minus):
        pl.semaphore_signal(barrier, inc=1, device_id=dev, device_id_type=MESH)

    for c in range(NC):
        xt[c, chip, k] = tok[c * T:(c + 1) * T, :].astype(F32).T.astype(BF16)

    pl.semaphore_wait(barrier, CH - 1 + 3)

    def rcopy(src, dst, ss, rs, dev):
        return pltpu.make_async_remote_copy(src_ref=src, dst_ref=dst, send_sem=ss, recv_sem=rs,
                                            device_id=dev, device_id_type=MESH)

    def a_send(c):
        def one(o, _):
            own = xt.at[c, chip, k]
            rcopy(own, own, a_s.at[c], a_r.at[c], (x, peer(o) * 2 + k)).start()
            return 0
        lax.fori_loop(1, CH, one, 0)

    def a_all(c):
        ref = xt.at[c, pl.ds(0, CH - 1), k]
        return rcopy(ref, ref, a_s.at[c], a_r.at[c], sibling)

    def a_pass(c):
        ref = xt.at[c, :, k]
        return rcopy(ref, ref, as_s.at[c], as_r.at[c], sibling)

    def x_copy(c, i):
        table = (
            (sg.at[c, xo], r1g.at[c], plus),
            (sg.at[c, xm], rpg.at[c], minus),
            (su.at[c, xp], rmu.at[c], plus),
            (su.at[c, xo], r1u.at[c], minus),
            (mg.at[c], rmg.at[c], plus),
            (mu.at[c], rpu.at[c], minus),
            (hb.at[c, x], hb.at[c, x], plus),
            (hb.at[c, x], hb.at[c, x], minus),
            (hb.at[c, xm, pl.ds(0, Q // 2)], hb.at[c, xm, pl.ds(0, Q // 2)], plus),
            (hb.at[c, xp, pl.ds(Q // 2, Q // 2)], hb.at[c, xp, pl.ds(Q // 2, Q // 2)], minus),
        )
        src, dst, dev = table[i]
        return rcopy(src, dst, x_s.at[c, i], x_r.at[c, i], dev)

    def x_recv(c, i):
        dst = (r1g.at[c], rpg.at[c], rmu.at[c], r1u.at[c], rmg.at[c], rpu.at[c],
               hb.at[c, xm], hb.at[c, xp],
               hb.at[c, xo, pl.ds(0, Q // 2)], hb.at[c, xo, pl.ds(Q // 2, Q // 2)])[i]
        rcopy(dst, dst, x_s.at[c, i], x_r.at[c, i], plus).wait_recv()

    def m1(c):
        a_all(c).wait_recv()
        a_pass(c).start()
        if c + 1 < NC:
            a_send(c + 1)
        if c == 0:
            weights[0].wait()
        a_in = xt.at[c, :, 1 - k]
        rcopy(a_in, a_in, as_s.at[c], as_r.at[c], sibling).wait_recv()
        for j in range(8):
            blk = xt[c, 2 * j:2 * j + 2].reshape(384, T)
            xn[:, 384 * j:384 * (j + 1)] = blk.astype(F32).T.astype(BF16)

        def half(w, pf, sb):
            @pl.loop(0, FL // 256)
            def _(j):
                cols = pl.ds(pl.multiple_of(j * 256, 256), 256)
                r = jnp.dot(xn[...], w[:, cols], preferred_element_type=F32)
                pf[c, :, cols] = r
                sb[c, :, :, cols] = r.astype(BF16).reshape(4, Q, 256)

        half(wg, pg, sg)
        x_copy(c, 0).start()
        x_copy(c, 1).start()
        if c == 0:
            weights[1].wait()
        half(wu, pu, su)
        x_copy(c, 2).start()
        x_copy(c, 3).start()

    def rows(q):
        return pl.ds(pl.multiple_of(q * Q, Q), Q)

    def relay(c):
        x_recv(c, 0)
        mg[c] = (pg[c, rows(xp), :] + r1g[c].astype(F32)).astype(BF16)
        x_copy(c, 4).start()
        x_recv(c, 3)
        mu[c] = (pu[c, rows(xm), :] + r1u[c].astype(F32)).astype(BF16)
        x_copy(c, 5).start()

    def act(c):
        x_recv(c, 1)
        x_recv(c, 2)
        x_recv(c, 4)
        x_recv(c, 5)
        gate = pg[c, rows(x), :] + rmg[c].astype(F32) + rpg[c].astype(F32)
        up = pu[c, rows(x), :] + rmu[c].astype(F32) + rpu[c].astype(F32)
        hb[c, x] = (gate / (1.0 + jnp.exp(-gate)) * up).astype(BF16)
        x_copy(c, 6).start()
        x_copy(c, 7).start()

    def forward(c):
        x_recv(c, 6)
        x_copy(c, 8).start()
        x_recv(c, 7)
        x_copy(c, 9).start()

    def d0(c):
        return rcopy(ob.at[c, :, 1 - k], sib.at[c], d0_s.at[c], d0_r.at[c], sibling)

    def m2(c):
        x_recv(c, 8)
        x_recv(c, 9)
        if c == 0:
            weights[2].wait()

        @pl.loop(0, 8)
        def _(j):
            cols = pl.ds(pl.multiple_of(j * 384, 384), 384)
            r = jnp.dot(hb[c].reshape(T, FL), wd[:, cols], preferred_element_type=F32)
            r = r.T
            of[pl.ds(2 * j, 2)] = r.reshape(2, 2, NB, T)
            ob[c, pl.ds(2 * j, 2)] = r.astype(BF16).reshape(2, 2, NB, T)

        d0(c).start()
        d0(c).wait_recv()
        s = of[:, k] + sib[c].astype(F32)
        sd[c] = s.astype(BF16)
        sf[c] = of[chip, k] + sib[c, chip].astype(F32)

        def one(o, _):
            q = peer(o)
            rcopy(sd.at[c, q], rd.at[c, o - 1], d1_s.at[c], d1_r.at[c], (x, q * 2 + k)).start()
            return 0
        lax.fori_loop(1, CH, one, 0)

    def d1_all(c):
        return rcopy(rd.at[c], rd.at[c], d1_s.at[c], d1_r.at[c], sibling)

    def finish(c):
        d1_all(c).wait_recv()
        total = sf[c]
        for o in range(CH - 1):
            total = total + rd[c, o].astype(F32)
        out[c * T:(c + 1) * T, :] = total.T.astype(BF16)

    a_send(0)
    for s in range(NC + 5):
        for off, step in ((0, m1), (1, relay), (2, act), (3, forward), (3, m2), (4, finish)):
            if 0 <= s - off < NC:
                step(s - off)

    for c in range(NC):
        a_all(c).wait_send()
        a_pass(c).wait_send()
        for i in range(10):
            x_copy(c, i).wait_send()
        d0(c).wait_send()
        d1_all(c).wait_send()


def body(tokens, gate_weight, up_weight, down_weight):
    vm = pltpu.VMEM
    dma = pltpu.SemaphoreType.DMA
    return pl.pallas_call(
        kernel,
        out_shape=jax.ShapeDtypeStruct((TOK, NB), BF16),
        in_specs=[pl.BlockSpec(memory_space=pltpu.VMEM)] + [pl.BlockSpec(memory_space=pl.ANY)] * 3,
        out_specs=pl.BlockSpec(memory_space=pltpu.VMEM),
        scratch_shapes=[
            vm((DL, FL), BF16), vm((DL, FL), BF16), vm((FL, DL), BF16),
            vm((NC, CH, 2, NB, T), BF16), vm((T, DL), BF16),
            vm((NC, T, FL), F32), vm((NC, T, FL), F32),
            vm((NC, 4, Q, FL), BF16), vm((NC, 4, Q, FL), BF16),
            vm((NC, Q, FL), BF16), vm((NC, Q, FL), BF16),
            vm((NC, Q, FL), BF16), vm((NC, Q, FL), BF16),
            vm((NC, Q, FL), BF16), vm((NC, Q, FL), BF16),
            vm((NC, Q, FL), BF16), vm((NC, Q, FL), BF16),
            vm((NC, 4, Q, FL), BF16),
            vm((NC, CH, 2, NB, T), BF16), vm((CH, 2, NB, T), F32),
            vm((NC, CH, NB, T), BF16), vm((NC, CH, NB, T), BF16),
            vm((NC, NB, T), F32), vm((NC, CH - 1, NB, T), BF16),
            dma((3,)), dma((NC,)), dma((NC,)), dma((NC,)), dma((NC,)),
            dma((NC, 10)), dma((NC, 10)), dma((NC,)), dma((NC,)), dma((NC,)), dma((NC,)),
        ],
        compiler_params=pltpu.CompilerParams(
            collective_id=0, has_side_effects=True, vmem_limit_bytes=60 * 2 ** 20
        ),
        cost_estimate=pl.CostEstimate(flops=12 * 10 ** 9, bytes_accessed=24 * 10 ** 6, transcendentals=0),
    )(tokens, gate_weight, up_weight, down_weight)


def solution(mesh):
    return jax.shard_map(
        body,
        mesh=mesh,
        in_specs=(P(None, ("gx", "yz")), P("gx", "yz"), P("gx", "yz"), P("yz", "gx")),
        out_specs=P(None, ("gx", "yz")),
        check_vma=False,
    )
```

time: 264 us -> 102 us (0.39)
  waiting for transfers between devices: 216 us -> 0 us
  Pallas kernels: 0 us -> 98.7 us
  matrix products: 26.2 us -> 0 us
  between operations: 13.2 us -> 0.01 us
  other arithmetic: 6.72 us -> 0 us
  local copies, waits for them, and re-layouts: 0.01 us -> 3.28 us
    reduce_scatter x2 -> x0, waiting for transfers between devices: 141 us -> none  [the longest x1 86.7 us: body(): mixed = lax.psum_scatter(partial_out, 'yz', scatter_dimension=1, tiled=True)]
    pallas_call x0 -> x1, Pallas kernels: none -> 98.7 us  [body(): pl.pallas_call(kernel, out_shape=jax.ShapeDtypeStruct((TOK, NB), BF16), i...]
    all_gather x2 -> x0, waiting for transfers between devices: 74.7 us -> none  [the longest x1 51.2 us: body(): features = lax.all_gather(tokens, 'yz', axis=1, tiled=True)]
    dot_general x3 -> x0, matrix products: 26.2 us -> none  [the longest x1 10.6 us: body(): jnp.dot(hidden, down_weight, preferred_element_type=jnp.float32)]
    convert_element_type x2 -> x0, other arithmetic: 3.78 us -> none  [the longest x1 2.2 us: body(): (jax.nn.silu(summed[:, :width]) * summed[:, width:]).astype(jnp.bfloat16)]
    concatenate x1 -> x0, other arithmetic: 2.94 us -> none  [body(): jnp.concatenate([gate_part, up_part], axis=1)]
  transfers between devices with their start and end apart: 4 -> 0, of which waited for: 4 -> 0; matrix products, arithmetic and copies ran while one was open for 0% -> 0% of each run, Pallas kernels for 0% -> 0%
where the time goes in v1:
time: 102 us
  Pallas kernels  98.7 us (97%)
  local copies, waits for them, and re-layouts  3.28 us (3%)
    pallas_call x1, Pallas kernels, body(): pl.pallas_call(kernel, out_shape=jax.ShapeDtypeStruct((TOK, NB), BF16), i...  98.7 us

profile of v1, /device:TPU:1, one launch (start us, length us, event | category | flops | bytes accessed | tf_op | source)
XLA Modules:
  0.0 102.0 jit_solution(8128999516309166004)
XLA Ops:
  0.0 1.6 %copy.5.tok = bf16[512,96]{1,0:T(8,128)(2,1)} copy(bf16[512,96]{0,1:T(8,128)(2,1)} %param.4) | data formatting | bytes 196608 | tf_op args[0]
  1.6 98.7 %shard_map.46 = bf16[512,96]{1,0:T(8,128)(2,1)} custom-call(bf16[512,96]{1,0:T(8,128)(2,1)} %copy.5.tok, bf16[3072,1280]{1,0:T(8,128)(2,1)} %wg_h.1, bf16[3072,1280]{1,0:T(8,128)(2,1)} %wu_h.1, bf16[1280,3072]{1,0:T(8,128)(2,1)} %wd_h.1), custom_call_target="tpu_custom_call" | custom-call | flops 12000000000 | bytes 24000000 | tf_op jit(solution)/shard_map/pallas_call | solution.py:217
  100.3 1.6 %copy.6 = bf16[512,96]{0,1:T(8,128)(2,1)} copy(bf16[512,96]{1,0:T(8,128)(2,1)} %shard_map.46) | data formatting | bytes 196608 | tf_op jit(solution)/shard_map/pallas_call | solution.py:217

commit v2 on v1

--- a/solution.py
+++ b/solution.py
@@ -20,7 +20,7 @@
 
 
 def kernel(tok, wg_h, wu_h, wd_h, out,
-           wg, wu, wd, xt, xn, pg, pu, sg, su, r1g, r1u, mg, mu, rmg, rmu, rpg, rpu,
+           wg, wu, wd, xt, pg, pu, sg, su, r1g, r1u, mg, mu, rmg, rmu, rpg, rpu,
            hb, ob, of, sib, sd, sf, rd,
            wsem, a_s, a_r, as_s, as_r, x_s, x_r, d0_s, d0_r, d1_s, d1_r):
     x = lax.axis_index("gx")
@@ -54,7 +54,7 @@
         pl.semaphore_signal(barrier, inc=1, device_id=dev, device_id_type=MESH)
 
     for c in range(NC):
-        xt[c, chip, k] = tok[c * T:(c + 1) * T, :].astype(F32).T.astype(BF16)
+        xt[c, chip, k] = tok[:, c * T:(c + 1) * T]
 
     pl.semaphore_wait(barrier, CH - 1 + 3)
 
@@ -99,43 +99,40 @@
                hb.at[c, xo, pl.ds(0, Q // 2)], hb.at[c, xo, pl.ds(Q // 2, Q // 2)])[i]
         rcopy(dst, dst, x_s.at[c, i], x_r.at[c, i], plus).wait_recv()
 
-    def m1(c):
+    def to_sibling(c):
         a_all(c).wait_recv()
         a_pass(c).start()
-        if c + 1 < NC:
-            a_send(c + 1)
+
+    def dot_in(c, w, pf, sb):
+        r = lax.dot_general(xt[c].reshape(DL, T), w[...], (((0,), (0,)), ((), ())), preferred_element_type=F32)
+        pf[c] = r
+        sb[c] = r.astype(BF16).reshape(4, Q, FL)
+
+    def m_gate(c):
+        a_in = xt.at[c, :, 1 - k]
+        rcopy(a_in, a_in, as_s.at[c], as_r.at[c], sibling).wait_recv()
         if c == 0:
             weights[0].wait()
-        a_in = xt.at[c, :, 1 - k]
-        rcopy(a_in, a_in, as_s.at[c], as_r.at[c], sibling).wait_recv()
-        for j in range(8):
-            blk = xt[c, 2 * j:2 * j + 2].reshape(384, T)
-            xn[:, 384 * j:384 * (j + 1)] = blk.astype(F32).T.astype(BF16)
-
-        def half(w, pf, sb):
-            @pl.loop(0, FL // 256)
-            def _(j):
-                cols = pl.ds(pl.multiple_of(j * 256, 256), 256)
-                r = jnp.dot(xn[...], w[:, cols], preferred_element_type=F32)
-                pf[c, :, cols] = r
-                sb[c, :, :, cols] = r.astype(BF16).reshape(4, Q, 256)
-
-        half(wg, pg, sg)
+        dot_in(c, wg, pg, sg)
         x_copy(c, 0).start()
         x_copy(c, 1).start()
+
+    def m_up(c):
         if c == 0:
             weights[1].wait()
-        half(wu, pu, su)
+        dot_in(c, wu, pu, su)
         x_copy(c, 2).start()
         x_copy(c, 3).start()
 
     def rows(q):
         return pl.ds(pl.multiple_of(q * Q, Q), Q)
 
-    def relay(c):
+    def r_gate(c):
         x_recv(c, 0)
         mg[c] = (pg[c, rows(xp), :] + r1g[c].astype(F32)).astype(BF16)
         x_copy(c, 4).start()
+
+    def r_up(c):
         x_recv(c, 3)
         mu[c] = (pu[c, rows(xm), :] + r1u[c].astype(F32)).astype(BF16)
         x_copy(c, 5).start()
@@ -166,19 +163,18 @@
         if c == 0:
             weights[2].wait()
 
-        @pl.loop(0, 8)
-        def _(j):
-            cols = pl.ds(pl.multiple_of(j * 384, 384), 384)
-            r = jnp.dot(hb[c].reshape(T, FL), wd[:, cols], preferred_element_type=F32)
-            r = r.T
-            of[pl.ds(2 * j, 2)] = r.reshape(2, 2, NB, T)
-            ob[c, pl.ds(2 * j, 2)] = r.astype(BF16).reshape(2, 2, NB, T)
-
+        n = DL // 2
+        for j in range(2):
+            r = jnp.dot(hb[c].reshape(T, FL), wd[:, j * n:(j + 1) * n], preferred_element_type=F32)
+            r = r.T.reshape(CH // 2, 2, NB, T)
+            of[c % 2, j * CH // 2:(j + 1) * CH // 2] = r
+            ob[c, j * CH // 2:(j + 1) * CH // 2] = r.astype(BF16)
         d0(c).start()
+
+    def scatter(c):
         d0(c).wait_recv()
-        s = of[:, k] + sib[c].astype(F32)
-        sd[c] = s.astype(BF16)
-        sf[c] = of[chip, k] + sib[c, chip].astype(F32)
+        sd[c] = (of[c % 2, :, k] + sib[c].astype(F32)).astype(BF16)
+        sf[c] = of[c % 2, chip, k] + sib[c, chip].astype(F32)
 
         def one(o, _):
             q = peer(o)
@@ -194,13 +190,18 @@
         total = sf[c]
         for o in range(CH - 1):
             total = total + rd[c, o].astype(F32)
-        out[c * T:(c + 1) * T, :] = total.T.astype(BF16)
-
-    a_send(0)
-    for s in range(NC + 5):
-        for off, step in ((0, m1), (1, relay), (2, act), (3, forward), (3, m2), (4, finish)):
-            if 0 <= s - off < NC:
-                step(s - off)
+        out[:, c * T:(c + 1) * T] = total.astype(BF16)
+
+    order = (
+        (a_send, 0), (a_send, 1), (a_send, 2), (to_sibling, 0), (m_gate, 0), (m_up, 0), (to_sibling, 1), (a_send, 3),
+        (m_gate, 1), (r_gate, 0), (m_up, 1), (r_up, 0), (to_sibling, 2), (m_gate, 2), (r_gate, 1), (r_up, 1), (m_up, 2),
+        (act, 0), (act, 1), (to_sibling, 3), (r_gate, 2), (r_up, 2), (forward, 0), (m_gate, 3), (m_up, 3),
+        (act, 2), (forward, 1), (m2, 0), (r_gate, 3), (r_up, 3), (scatter, 0), (forward, 2), (m2, 1), (act, 3),
+        (scatter, 1), (m2, 2), (forward, 3), (scatter, 2), (m2, 3), (scatter, 3),
+        (finish, 0), (finish, 1), (finish, 2), (finish, 3),
+    )
+    for step, c in order:
+        step(c)
 
     for c in range(NC):
         a_all(c).wait_send()
@@ -216,12 +217,12 @@
     dma = pltpu.SemaphoreType.DMA
     return pl.pallas_call(
         kernel,
-        out_shape=jax.ShapeDtypeStruct((TOK, NB), BF16),
+        out_shape=jax.ShapeDtypeStruct((NB, TOK), BF16),
         in_specs=[pl.BlockSpec(memory_space=pltpu.VMEM)] + [pl.BlockSpec(memory_space=pl.ANY)] * 3,
         out_specs=pl.BlockSpec(memory_space=pltpu.VMEM),
         scratch_shapes=[
             vm((DL, FL), BF16), vm((DL, FL), BF16), vm((FL, DL), BF16),
-            vm((NC, CH, 2, NB, T), BF16), vm((T, DL), BF16),
+            vm((NC, CH, 2, NB, T), BF16),
             vm((NC, T, FL), F32), vm((NC, T, FL), F32),
             vm((NC, 4, Q, FL), BF16), vm((NC, 4, Q, FL), BF16),
             vm((NC, Q, FL), BF16), vm((NC, Q, FL), BF16),
@@ -229,7 +230,7 @@
             vm((NC, Q, FL), BF16), vm((NC, Q, FL), BF16),
             vm((NC, Q, FL), BF16), vm((NC, Q, FL), BF16),
             vm((NC, 4, Q, FL), BF16),
-            vm((NC, CH, 2, NB, T), BF16), vm((CH, 2, NB, T), F32),
+            vm((NC, CH, 2, NB, T), BF16), vm((2, CH, 2, NB, T), F32),
             vm((NC, CH, NB, T), BF16), vm((NC, CH, NB, T), BF16),
             vm((NC, NB, T), F32), vm((NC, CH - 1, NB, T), BF16),
             dma((3,)), dma((NC,)), dma((NC,)), dma((NC,)), dma((NC,)),
@@ -239,7 +240,7 @@
             collective_id=0, has_side_effects=True, vmem_limit_bytes=60 * 2 ** 20
         ),
         cost_estimate=pl.CostEstimate(flops=12 * 10 ** 9, bytes_accessed=24 * 10 ** 6, transcendentals=0),
-    )(tokens, gate_weight, up_weight, down_weight)
+    )(tokens.T, gate_weight, up_weight, down_weight).T
 
 
 def solution(mesh):

time: 102 us -> 73.9 us (0.72)
  Pallas kernels: 98.7 us -> 72.2 us
  local copies, waits for them, and re-layouts: 3.28 us -> 1.54 us
    pallas_call x1, Pallas kernels: 98.7 us -> 72.2 us  [body(): pl.pallas_call(kernel, out_shape=jax.ShapeDtypeStruct((NB, TOK), BF16), i...]
    pallas_call x1 -> x0, local copies, waits for them, and re-layouts: 1.64 us -> none  [body(): pl.pallas_call(kernel, out_shape=jax.ShapeDtypeStruct((TOK, NB), BF16), i...]
where the time goes in v2:
time: 73.9 us; the launch traced here: 73.8 us
  Pallas kernels  72.2 us (98%)
  local copies, waits for them, and re-layouts  1.54 us (2%)
    pallas_call x1, Pallas kernels, body(): pl.pallas_call(kernel, out_shape=jax.ShapeDtypeStruct((NB, TOK), BF16), i...  72.2 us
    unnamed x1, local copies, waits for them, and re-layouts  1.54 us

profile of v2, /device:TPU:1, one launch (start us, length us, event | category | flops | bytes accessed | tf_op | source)
XLA Modules:
  0.0 73.8 jit_solution(10702832330371577769)
XLA Ops:
  0.0 72.2 %shard_map.46 = bf16[96,512]{1,0:T(8,128)(2,1)} custom-call(bf16[96,512]{1,0:T(8,128)(2,1)} %bitcast.3, bf16[3072,1280]{1,0:T(8,128)(2,1)} %wg_h.1, bf16[3072,1280]{1,0:T(8,128)(2,1)} %wu_h.1, bf16[1280,3072]{1,0:T(8,128)(2,1)} %wd_h.1), custom_call_target="tpu_custom_call" | custom-call | flops 12000000000 | bytes 24000000 | tf_op jit(solution)/shard_map/pallas_call | solution.py:218
  72.2 1.5 %copy.6 = bf16[512,96]{0,1:T(8,128)(2,1)} copy(bf16[512,96]{0,1:T(8,128)(2,1)} %bitcast.2) | data formatting | bytes 196608

commit v3 on v0

v3 whole, which is shorter than its diff:
```python
import jax
import jax.numpy as jnp
from jax import lax
from jax.experimental import pallas as pl
from jax.experimental.pallas import tpu as pltpu
from jax.sharding import PartitionSpec as P

MESH = pl.DeviceIdType.MESH
F32 = jnp.float32
BF16 = jnp.bfloat16

TOK = 512
NC = 4
T = TOK // NC
Q = T // 4
DL = 3072
FL = 1280
NB = 96
CH = 16
ROW = 4 * 2 * NB

PARTS = (((0, 1280),), ((0, 1280),), ((0, 1280),), ((0, 768), (768, 512)))
MAXP = max(len(p) for p in PARTS)
STRAIGHT = (3,)


def kernel(tok, wg_h, wu_h, wd_h, out,
           wg, wu, wd, xt, pg, pu, sg, su, r1g, r1u, mg, mu, rmg, rmu, rpg, rpu,
           hb, ob, of, sib, sd, sf, rd, ot,
           wsem, t_s, o_s, a_s, a_r, as_s, as_r, x_s, x_r, d0_s, d0_r, d1_s, d1_r):
    x = lax.axis_index("gx")
    yz = lax.axis_index("yz")
    chip = yz // 2
    k = yz % 2
    y = chip // 4
    z = chip % 4
    xp = (x + 1) % 4
    xm = (x + 3) % 4
    xo = (x + 2) % 4
    sibling = (x, chip * 2 + (1 - k))
    plus = (xp, yz)
    minus = (xm, yz)
    opposite = (xo, yz)

    def peer(dy, dz):
        return ((y + dy) % 4) * 4 + (z + dz) % 4

    far_first = [(dy, dz) for dy in (2, 1, 3, 0) for dz in (2, 1, 3, 0) if dy or dz]
    far_first.sort(key=lambda d: -min(d[0], 4 - d[0]) - min(d[1], 4 - d[1]))

    barrier = pltpu.get_barrier_semaphore()
    for dy, dz in far_first:
        pl.semaphore_signal(barrier, inc=1, device_id=(x, peer(dy, dz) * 2 + k), device_id_type=MESH)
    for dev in (opposite, plus, minus, sibling):
        pl.semaphore_signal(barrier, inc=1, device_id=dev, device_id_type=MESH)

    own_tokens = [pltpu.make_async_copy(tok.at[:, pl.ds(c * T, T)], xt.at[c, k, chip], t_s.at[c]) for c in range(NC)]
    weights = [pltpu.make_async_copy(h, v, wsem.at[i]) for i, (h, v) in enumerate(((wg_h, wg), (wu_h, wu), (wd_h, wd)))]
    for copy in own_tokens + weights:
        copy.start()

    pl.semaphore_wait(barrier, CH - 1 + 4)

    def rcopy(src, dst, ss, rs, dev):
        return pltpu.make_async_remote_copy(src_ref=src, dst_ref=dst, send_sem=ss, recv_sem=rs,
                                            device_id=dev, device_id_type=MESH)

    pending = []

    def start(copy):
        copy.start()
        pending.append(copy)

    def a_send(c):
        own_tokens[c].wait()
        own = xt.at[c, k, chip]
        for dy, dz in far_first:
            rcopy(own, own, a_s.at[c], a_r.at[c], (x, peer(dy, dz) * 2 + k)).start()
        pending.append(a_all(c))

    def a_all(c):
        ref = xt.at[c, k, pl.ds(0, CH - 1)]
        return rcopy(ref, ref, a_s.at[c], a_r.at[c], sibling)

    def a_pass(c):
        ref = xt.at[c, k]
        return rcopy(ref, ref, as_s.at[c], as_r.at[c], sibling)

    def to_sibling(c):
        a_all(c).wait_recv()
        start(a_pass(c))

    def x_copy(c, p, i):
        s, w = PARTS[c][p]
        cols = pl.ds(s, w)
        hx = hb.at[c, x, :, cols]
        if i == 8 and c in STRAIGHT:
            src, dst, dev = hx, hx, opposite
        else:
            lo = hb.at[c, xm, pl.ds(0, Q // 2), cols]
            hi = hb.at[c, xp, pl.ds(Q // 2, Q // 2), cols]
            src, dst, dev = (
                (sg.at[c, xo, :, cols], r1g.at[c, :, cols], plus),
                (sg.at[c, xm, :, cols], rpg.at[c, :, cols], minus),
                (su.at[c, xp, :, cols], rmu.at[c, :, cols], plus),
                (su.at[c, xo, :, cols], r1u.at[c, :, cols], minus),
                (mg.at[c, :, cols], rmg.at[c, :, cols], plus),
                (mu.at[c, :, cols], rpu.at[c, :, cols], minus),
                (hx, hx, plus),
                (hx, hx, minus),
                (lo, lo, plus),
                (hi, hi, minus),
            )[i]
        return rcopy(src, dst, x_s.at[c, p, i], x_r.at[c, p, i], dev)

    def x_recv(c, p, i):
        s, w = PARTS[c][p]
        cols = pl.ds(s, w)
        if i == 8 and c in STRAIGHT:
            dst = hb.at[c, xo, :, cols]
        else:
            dst = (r1g.at[c, :, cols], rpg.at[c, :, cols], rmu.at[c, :, cols], r1u.at[c, :, cols],
                   rmg.at[c, :, cols], rpu.at[c, :, cols], hb.at[c, xm, :, cols], hb.at[c, xp, :, cols],
                   hb.at[c, xo, pl.ds(0, Q // 2), cols], hb.at[c, xo, pl.ds(Q // 2, Q // 2), cols])[i]
        rcopy(dst, dst, x_s.at[c, p, i], x_r.at[c, p, i], plus).wait_recv()

    def dot_in(c, core, w, s, n):
        return lax.dot_general(xt[c, core].reshape(DL // 2, T), w[:, core, :, s:s + n].reshape(DL // 2, n),
                               (((0,), (0,)), ((), ())), preferred_element_type=F32)

    def m_own(c):
        if c == 0:
            weights[0].wait()
        pg[c] = dot_in(c, k, wg, 0, FL)
        if c == 0:
            weights[1].wait()
        pu[c] = dot_in(c, k, wu, 0, FL)

    def m_gate(c, p):
        if p == 0:
            a_in = xt.at[c, 1 - k]
            rcopy(a_in, a_in, as_s.at[c], as_r.at[c], sibling).wait_recv()
        s, n = PARTS[c][p]
        r = pg[c, :, s:s + n] + dot_in(c, 1 - k, wg, s, n)
        pg[c, :, s:s + n] = r
        sg[c, :, :, s:s + n] = r.astype(BF16).reshape(4, Q, n)
        start(x_copy(c, p, 0))
        start(x_copy(c, p, 1))

    def m_up(c, p):
        s, n = PARTS[c][p]
        r = pu[c, :, s:s + n] + dot_in(c, 1 - k, wu, s, n)
        pu[c, :, s:s + n] = r
        su[c, :, :, s:s + n] = r.astype(BF16).reshape(4, Q, n)
        start(x_copy(c, p, 2))
        start(x_copy(c, p, 3))

    def rows(q):
        return pl.ds(pl.multiple_of(q * Q, Q), Q)

    def r_gate(c, p):
        s, n = PARTS[c][p]
        x_recv(c, p, 0)
        mg[c, :, s:s + n] = (pg[c, rows(xp), s:s + n] + r1g[c, :, s:s + n].astype(F32)).astype(BF16)
        start(x_copy(c, p, 4))

    def r_up(c, p):
        s, n = PARTS[c][p]
        x_recv(c, p, 3)
        mu[c, :, s:s + n] = (pu[c, rows(xm), s:s + n] + r1u[c, :, s:s + n].astype(F32)).astype(BF16)
        start(x_copy(c, p, 5))

    def act(c, p):
        s, n = PARTS[c][p]
        for i in (1, 2, 4, 5):
            x_recv(c, p, i)
        gate = pg[c, rows(x), s:s + n] + rmg[c, :, s:s + n].astype(F32) + rpg[c, :, s:s + n].astype(F32)
        up = pu[c, rows(x), s:s + n] + rmu[c, :, s:s + n].astype(F32) + rpu[c, :, s:s + n].astype(F32)
        hb[c, x, :, s:s + n] = (gate / (1.0 + jnp.exp(-gate)) * up).astype(BF16)
        for i in (8, 6, 7) if c in STRAIGHT else (6, 7):
            start(x_copy(c, p, i))

    def forward(c, p):
        if c not in STRAIGHT:
            x_recv(c, p, 6)
            start(x_copy(c, p, 8))
            x_recv(c, p, 7)
            start(x_copy(c, p, 9))

    halves = ((2, 0), (1, 3))

    def d0(c, dy):
        chips = pl.ds(4 * ((y + dy) % 4), 4)
        return rcopy(ob.at[c, 1 - k, chips], sib.at[c, chips], d0_s.at[c, dy], d0_r.at[c, dy], sibling)

    def m2(c, j):
        if j == 0:
            for p in range(len(PARTS[c])):
                for i in (6, 7, 8) if c in STRAIGHT else (8, 9):
                    x_recv(c, p, i)
            if c == 0:
                weights[2].wait()
        for dy in halves[j]:
            yd = (y + dy) % 4
            cols = pl.ds(pl.multiple_of(yd * ROW, ROW), ROW)
            r = jnp.dot(hb[c].reshape(T, FL), wd[:, cols], preferred_element_type=F32)
            r = r.T.reshape(4, 2, NB, T)
            chips = pl.ds(4 * yd, 4)
            for core in range(2):
                of[c % 2, core, chips] = r[:, core]
                ob[c, core, chips] = r[:, core].astype(BF16)
            start(d0(c, dy))

    def scatter(c, j):
        for dy in halves[j]:
            d0(c, dy).wait_recv()
            chips = pl.ds(4 * ((y + dy) % 4), 4)
            sd[c, chips] = (of[c % 2, k, chips] + sib[c, chips].astype(F32)).astype(BF16)
            if dy == 0:
                sf[c] = of[c % 2, k, chip] + sib[c, chip].astype(F32)
            for dz in (2, 1, 3, 0):
                if dy or dz:
                    q = peer(dy, dz)
                    rcopy(sd.at[c, q], rd.at[c, 4 * dy + dz - 1], d1_s.at[c], d1_r.at[c], (x, q * 2 + k)).start()
        if j == 1:
            pending.append(d1_all(c))

    def d1_all(c):
        return rcopy(rd.at[c], rd.at[c], d1_s.at[c], d1_r.at[c], sibling)

    def finish(c):
        d1_all(c).wait_recv()
        total = sf[c]
        for o in range(CH - 1):
            total = total + rd[c, o].astype(F32)
        ot[c] = total.astype(BF16)
        done = pltpu.make_async_copy(ot.at[c], out.at[:, pl.ds(c * T, T)], o_s.at[c])
        done.start()
        finished.append(done)

    finished = []
    order = (
        (a_send, 0), (a_send, 1), (a_send, 2), (to_sibling, 0), (m_own, 0), (m_gate, 0, 0), (m_up, 0, 0),
        (to_sibling, 1), (m_own, 1), (m_gate, 1, 0), (a_send, 3), (m_up, 1, 0), (r_gate, 0, 0), (r_up, 0, 0),
        (to_sibling, 2), (m_own, 2), (m_gate, 2, 0), (r_gate, 1, 0), (r_up, 1, 0), (to_sibling, 3), (act, 0, 0),
        (m_up, 2, 0), (m_own, 3), (m_gate, 3, 0), (forward, 0, 0), (act, 1, 0), (r_gate, 2, 0), (r_up, 2, 0),
        (m_up, 3, 0), (m2, 0, 0), (forward, 1, 0), (m_gate, 3, 1), (m_up, 3, 1), (m2, 0, 1), (act, 2, 0),
        (scatter, 0, 0), (scatter, 0, 1), (r_gate, 3, 0), (r_up, 3, 0), (r_up, 3, 1), (r_gate, 3, 1), (m2, 1, 0),
        (forward, 2, 0), (m2, 1, 1), (act, 3, 0), (scatter, 1, 0), (scatter, 1, 1), (act, 3, 1), (m2, 2, 0),
        (m2, 2, 1), (scatter, 2, 0), (scatter, 2, 1), (m2, 3, 0), (m2, 3, 1), (scatter, 3, 0), (finish, 1),
        (scatter, 3, 1), (finish, 2), (finish, 0), (finish, 3),
    )
    for step, *where in order:
        step(*where)

    for copy in pending:
        copy.wait_send()
    for copy in finished:
        copy.wait()


def body(tokens, gate_weight, up_weight, down_weight):
    vm = pltpu.VMEM
    dma = pltpu.SemaphoreType.DMA
    return pl.pallas_call(
        kernel,
        out_shape=jax.ShapeDtypeStruct((NB, TOK), BF16),
        in_specs=[pl.BlockSpec(memory_space=pl.ANY)] * 4,
        out_specs=pl.BlockSpec(memory_space=pl.ANY),
        scratch_shapes=[
            vm((CH, 2, NB, FL), BF16), vm((CH, 2, NB, FL), BF16), vm((FL, DL), BF16),
            vm((NC, 2, CH, NB, T), BF16),
            vm((NC, T, FL), F32), vm((NC, T, FL), F32),
            vm((NC, 4, Q, FL), BF16), vm((NC, 4, Q, FL), BF16),
            vm((NC, Q, FL), BF16), vm((NC, Q, FL), BF16),
            vm((NC, Q, FL), BF16), vm((NC, Q, FL), BF16),
            vm((NC, Q, FL), BF16), vm((NC, Q, FL), BF16),
            vm((NC, Q, FL), BF16), vm((NC, Q, FL), BF16),
            vm((NC, 4, Q, FL), BF16),
            vm((NC, 2, CH, NB, T), BF16), vm((2, 2, CH, NB, T), F32),
            vm((NC, CH, NB, T), BF16), vm((NC, CH, NB, T), BF16),
            vm((NC, NB, T), F32), vm((NC, CH - 1, NB, T), BF16), vm((NC, NB, T), BF16),
            dma((3,)), dma((NC,)), dma((NC,)), dma((NC,)), dma((NC,)), dma((NC,)), dma((NC,)),
            dma((NC, MAXP, 10)), dma((NC, MAXP, 10)), dma((NC, 4)), dma((NC, 4)), dma((NC,)), dma((NC,)),
        ],
        compiler_params=pltpu.CompilerParams(
            collective_id=0, has_side_effects=True, vmem_limit_bytes=60 * 2 ** 20
        ),
        cost_estimate=pl.CostEstimate(flops=12 * 10 ** 9, bytes_accessed=24 * 10 ** 6, transcendentals=0),
    )(tokens.T, gate_weight.reshape(CH, 2, NB, FL), up_weight.reshape(CH, 2, NB, FL), down_weight).T


def solution(mesh):
    return jax.shard_map(
        body,
        mesh=mesh,
        in_specs=(P(None, ("gx", "yz")), P("gx", "yz"), P("gx", "yz"), P("yz", "gx")),
        out_specs=P(None, ("gx", "yz")),
        check_vma=False,
    )
```

time: 264 us -> 69.9 us (0.26)
  waiting for transfers between devices: 216 us -> 0 us
  Pallas kernels: 0 us -> 68.2 us
  matrix products: 26.2 us -> 0 us
  between operations: 13.2 us -> 0.01 us
  other arithmetic: 6.72 us -> 0 us
    reduce_scatter x2 -> x0, waiting for transfers between devices: 141 us -> none  [the longest x1 86.7 us: body(): mixed = lax.psum_scatter(partial_out, 'yz', scatter_dimension=1, tiled=True)]
    all_gather x2 -> x0, waiting for transfers between devices: 74.7 us -> none  [the longest x1 51.2 us: body(): features = lax.all_gather(tokens, 'yz', axis=1, tiled=True)]
    pallas_call x0 -> x1, Pallas kernels: none -> 68.2 us  [body(): pl.pallas_call(kernel, out_shape=jax.ShapeDtypeStruct((NB, TOK), BF16), i...]
    dot_general x3 -> x0, matrix products: 26.2 us -> none  [the longest x1 10.6 us: body(): jnp.dot(hidden, down_weight, preferred_element_type=jnp.float32)]
    convert_element_type x2 -> x0, other arithmetic: 3.78 us -> none  [the longest x1 2.2 us: body(): (jax.nn.silu(summed[:, :width]) * summed[:, width:]).astype(jnp.bfloat16)]
    concatenate x1 -> x0, other arithmetic: 2.94 us -> none  [body(): jnp.concatenate([gate_part, up_part], axis=1)]
  transfers between devices with their start and end apart: 4 -> 0, of which waited for: 4 -> 0; matrix products, arithmetic and copies ran while one was open for 0% -> 0% of each run, Pallas kernels for 0% -> 0%
where the time goes in v3:
time: 69.9 us; the launch traced here: 69.8 us
  Pallas kernels  68.2 us (98%)
  local copies, waits for them, and re-layouts  1.54 us (2%)
    pallas_call x1, Pallas kernels, body(): pl.pallas_call(kernel, out_shape=jax.ShapeDtypeStruct((NB, TOK), BF16), i...  68.2 us
    unnamed x1, local copies, waits for them, and re-layouts  1.54 us

profile of v3, /device:TPU:1, one launch (start us, length us, event | category | flops | bytes accessed | tf_op | source)
XLA Modules:
  0.0 69.8 jit_solution(6738709444799474263)
XLA Ops:
  0.0 68.2 %shard_map.46 = bf16[96,512]{1,0:T(8,128)(2,1)} custom-call(bf16[96,512]{1,0:T(8,128)(2,1)} %bitcast.7, bf16[16,2,96,1280]{3,2,1,0:T(8,128)(2,1)} %bitcast.5, bf16[16,2,96,1280]{3,2,1,0:T(8,128)(2,1)} %bitcast.6, bf16[1280,3072]{1,0:T(8,128)(2,1)} %wd_h.1), custom_call_target="tpu_custom_call" | custom-call | flops 12000000000 | bytes 24000000 | tf_op jit(solution)/shard_map/pallas_call | solution.py:265
  68.2 1.5 %copy.6 = bf16[512,96]{0,1:T(8,128)(2,1)} copy(bf16[512,96]{0,1:T(8,128)(2,1)} %bitcast.4) | data formatting | bytes 196608

commit v4 on v3

--- a/solution.py
+++ b/solution.py
@@ -42,15 +42,16 @@
     minus = (xm, yz)
     opposite = (xo, yz)
 
-    def peer(dy, dz):
-        return ((y + dy) % 4) * 4 + (z + dz) % 4
+    row = [y] + [(y + d) % 4 for d in (1, 2, 3)]
+    col = [z] + [(z + d) % 4 for d in (1, 2, 3)]
+    peer = [[(x, row[dy] * 8 + col[dz] * 2 + k) for dz in range(4)] for dy in range(4)]
 
     far_first = [(dy, dz) for dy in (2, 1, 3, 0) for dz in (2, 1, 3, 0) if dy or dz]
     far_first.sort(key=lambda d: -min(d[0], 4 - d[0]) - min(d[1], 4 - d[1]))
 
     barrier = pltpu.get_barrier_semaphore()
     for dy, dz in far_first:
-        pl.semaphore_signal(barrier, inc=1, device_id=(x, peer(dy, dz) * 2 + k), device_id_type=MESH)
+        pl.semaphore_signal(barrier, inc=1, device_id=peer[dy][dz], device_id_type=MESH)
     for dev in (opposite, plus, minus, sibling):
         pl.semaphore_signal(barrier, inc=1, device_id=dev, device_id_type=MESH)
 
@@ -75,7 +76,7 @@
         own_tokens[c].wait()
         own = xt.at[c, k, chip]
         for dy, dz in far_first:
-            rcopy(own, own, a_s.at[c], a_r.at[c], (x, peer(dy, dz) * 2 + k)).start()
+            rcopy(own, own, a_s.at[c], a_r.at[c], peer[dy][dz]).start()
         pending.append(a_all(c))
 
     def a_all(c):
@@ -216,13 +217,14 @@
             d0(c, dy).wait_recv()
             chips = pl.ds(4 * ((y + dy) % 4), 4)
             sd[c, chips] = (of[c % 2, k, chips] + sib[c, chips].astype(F32)).astype(BF16)
-            if dy == 0:
-                sf[c] = of[c % 2, k, chip] + sib[c, chip].astype(F32)
-            for dz in (2, 1, 3, 0):
+        for dz in (2, 1, 3, 0):
+            for dy in halves[j]:
                 if dy or dz:
-                    q = peer(dy, dz)
-                    rcopy(sd.at[c, q], rd.at[c, 4 * dy + dz - 1], d1_s.at[c], d1_r.at[c], (x, q * 2 + k)).start()
-        if j == 1:
+                    q = row[dy] * 4 + col[dz]
+                    rcopy(sd.at[c, q], rd.at[c, 4 * dy + dz - 1], d1_s.at[c], d1_r.at[c], peer[dy][dz]).start()
+        if j == 0:
+            sf[c] = of[c % 2, k, chip] + sib[c, chip].astype(F32)
+        else:
             pending.append(d1_all(c))
 
     def d1_all(c):
@@ -240,7 +242,7 @@
 
     finished = []
     order = (
-        (a_send, 0), (a_send, 1), (a_send, 2), (to_sibling, 0), (m_own, 0), (m_gate, 0, 0), (m_up, 0, 0),
+        (a_send, 0), (a_send, 1), (to_sibling, 0), (a_send, 2), (m_own, 0), (m_gate, 0, 0), (m_up, 0, 0),
         (to_sibling, 1), (m_own, 1), (m_gate, 1, 0), (a_send, 3), (m_up, 1, 0), (r_gate, 0, 0), (r_up, 0, 0),
         (to_sibling, 2), (m_own, 2), (m_gate, 2, 0), (r_gate, 1, 0), (r_up, 1, 0), (to_sibling, 3), (act, 0, 0),
         (m_up, 2, 0), (m_own, 3), (m_gate, 3, 0), (forward, 0, 0), (act, 1, 0), (r_gate, 2, 0), (r_up, 2, 0),

time: 69.9 us -> 70.3 us (level)
  no operation moved by 1% of the time
where the time goes in v4:
time: 70.3 us; the launch traced here: 70.1 us
  Pallas kernels  68.6 us (98%)
  local copies, waits for them, and re-layouts  1.54 us (2%)
    pallas_call x1, Pallas kernels, body(): pl.pallas_call(kernel, out_shape=jax.ShapeDtypeStruct((NB, TOK), BF16), i...  68.6 us
    unnamed x1, local copies, waits for them, and re-layouts  1.54 us

profile of v4, /device:TPU:1, one launch (start us, length us, event | category | flops | bytes accessed | tf_op | source)
XLA Modules:
  0.0 70.1 jit_solution(14433605812062754076)
XLA Ops:
  0.0 68.6 %shard_map.46 = bf16[96,512]{1,0:T(8,128)(2,1)} custom-call(bf16[96,512]{1,0:T(8,128)(2,1)} %bitcast.7, bf16[16,2,96,1280]{3,2,1,0:T(8,128)(2,1)} %bitcast.5, bf16[16,2,96,1280]{3,2,1,0:T(8,128)(2,1)} %bitcast.6, bf16[1280,3072]{1,0:T(8,128)(2,1)} %wd_h.1), custom_call_target="tpu_custom_call" | custom-call | flops 12000000000 | bytes 24000000 | tf_op jit(solution)/shard_map/pallas_call | solution.py:267
  68.6 1.5 %copy.6 = bf16[512,96]{0,1:T(8,128)(2,1)} copy(bf16[512,96]{0,1:T(8,128)(2,1)} %bitcast.4) | data formatting | bytes 196608
